TPU v7x, 32 devices: a whole 2x2x4 slice. The times are simulated.
32 devices in a mesh: group: 2 (over y), gx: 4 (over z), gz: 2 (over x), col: 2 (over core).
Axes of the slice: x: 2, y: 2, z: 4, core: 2. Of those that a mesh axis runs over, the one named last changes fastest.
Arguments:
- features: bfloat16 [32, 64, 16, 256], P(None, 'col', ('group', 'gx'), 'gz'), parts along dimension 2, may hold values from -6 to 6
- labels: int32 [64, 16, 256], P(None, ('group', 'gx'), 'gz'), parts along dimension 1, may hold values from 0 to 3
- grid_index: int32 [64], replicated, may hold values from 0 to 15
- stretch: float32 [16, 9], replicated, may hold values from 0.5 to 2
- tile_filter: float32 [32, 25], replicated, may hold values from -1.25 to 1.25
- wall_filter: float32 [32, 9], replicated, may hold values from -2 to 2
- class_weight: float32 [4, 32], replicated, may hold values from -1 to 1
Outputs:
- grad_features: bfloat16 [32, 64, 16, 256], P(None, 'col', ('group', 'gx'), 'gz'), parts along dimension 2
- grad_tile_filter: float32 [64, 25], P('group'), parts along dimension 0
- grad_wall_filter: float32 [64, 9], P('group'), parts along dimension 0
- grad_class_weight: float32 [8, 32], P('group'), parts along dimension 0
There are 2 independent parts, one for each index of `group`. A program takes and returns all parts, laid end to end along the dimension named above; an argument that names none is the same for every part. Nothing has to cross between parts.
All inputs are finite; a program needn't handle non-finite values.
Results may differ from a plain program's by a relative error of at most 0.0064.
Values may be sent and summed in bfloat16 or wider, within the bound.
A program may use at most 64 MiB of HBM per device.

v0:
```python
import jax
import jax.numpy as jnp
from jax import lax
from jax.sharding import PartitionSpec as P


def with_halo(value, sides, width):
    for axis, dim in sides:
        size, length = (lax.axis_size(axis), value.shape[dim])
        up = [(i, (i + 1) % size) for i in range(size)]
        down = [(j, i) for i, j in up]
        last = lax.slice_in_dim(value, length - width, length, axis=dim)
        leading = lax.slice_in_dim(value, 0, width, axis=dim)
        before = lax.ppermute(last, axis, up)
        after = lax.ppermute(leading, axis, down)
        value = jnp.concatenate([before, value, after], axis=dim)
    return value


def rim_tiles(field):
    return with_halo(field, (("gx", 2), ("gz", 3)), 2)


def band_table(grid_index, stretch):
    levels = stretch.shape[0]
    onehot = (grid_index[:, None] == jnp.arange(levels, dtype=jnp.int32)[None, :]).astype(
        jnp.float32
    )
    return jnp.dot(onehot, stretch, precision=lax.Precision.HIGHEST)


def wall_forward(smooth_ext, wall_rows, band_rows):
    rows = band_rows.shape[0]
    total = jnp.zeros((smooth_ext.shape[0], rows) + smooth_ext.shape[2:], jnp.float32)
    for k in range(9):
        tap = wall_rows[:, k][:, None] * band_rows[:, k][None, :]
        total = total + tap[:, :, None, None] * smooth_ext[:, k : k + rows].astype(jnp.float32)
    return total


def wall_backward(grad_ext, wall_rows, band_ext, rows):
    total = jnp.zeros((grad_ext.shape[0], rows) + grad_ext.shape[2:], jnp.float32)
    for k in range(9):
        first = 8 - k
        tap = wall_rows[:, k][:, None] * band_ext[first : first + rows, k][None, :]
        total = total + tap[:, :, None, None] * grad_ext[:, first : first + rows].astype(
            jnp.float32
        )
    return total


def shards(features, labels, grid_index, stretch, tile_filter, wall_filter, class_weight):
    chans, half_rows, cells_x, cells_z = features.shape
    all_rows = labels.shape[0]
    classes = class_weight.shape[0]
    volume = all_rows * cells_x * lax.axis_size("gx") * cells_z * lax.axis_size("gz")
    widened = rim_tiles(features)
    smooth = jnp.zeros(features.shape, jnp.float32)
    for i in range(5):
        for j in range(5):
            weight = tile_filter[:, 5 * i + j][:, None, None, None]
            smooth = smooth + weight * widened[:, :, i : i + cells_x, j : j + cells_z].astype(
                jnp.float32
            )
    smoothed = smooth.astype(jnp.bfloat16)
    bands = band_table(grid_index, stretch)
    bands_pad = jnp.pad(bands, ((4, 4), (0, 0)))
    place = lax.axis_index("col")
    share = chans // lax.axis_size("col")
    first_chan = place * share
    pencil = lax.all_to_all(smoothed, "col", split_axis=0, concat_axis=1, tiled=True)
    smooth_ext = jnp.pad(pencil, ((0, 0), (4, 4), (0, 0), (0, 0)))
    wall_rows = lax.dynamic_slice_in_dim(wall_filter, first_chan, share, 0)
    class_rows = lax.dynamic_slice_in_dim(class_weight, first_chan, share, 1)
    wall_out = wall_forward(smooth_ext, wall_rows, bands)
    sig = jax.nn.sigmoid(wall_out)
    hidden = wall_out * sig
    partial_scores = jnp.einsum(
        "kc,cyxz->kyxz", class_rows, hidden, precision=lax.Precision.HIGHEST
    )
    scores = lax.psum(partial_scores, "col")
    targets = (labels[None] == jnp.arange(classes, dtype=jnp.int32)[:, None, None, None]).astype(
        jnp.float32
    )
    errors = scores - targets
    grad_hidden = jnp.einsum("kc,kyxz->cyxz", class_rows, errors, precision=lax.Precision.HIGHEST)
    grad_wall = (grad_hidden * sig * (1.0 + wall_out * (1.0 - sig))).astype(jnp.bfloat16)
    class_part = jnp.einsum("kyxz,cyxz->kc", errors, hidden, precision=lax.Precision.HIGHEST)
    grad_vals = grad_wall.astype(jnp.float32)
    wall_part = jnp.stack(
        [
            jnp.sum(
                grad_vals
                * bands[:, k][None, :, None, None]
                * smooth_ext[:, k : k + all_rows].astype(jnp.float32),
                axis=(1, 2, 3),
            )
            for k in range(9)
        ],
        axis=1,
    )
    grad_ext = jnp.pad(grad_wall, ((0, 0), (4, 4), (0, 0), (0, 0)))
    grad_smooth = wall_backward(grad_ext, wall_rows, bands_pad, all_rows).astype(jnp.bfloat16)
    grad_tile = lax.all_to_all(grad_smooth, "col", split_axis=1, concat_axis=0, tiled=True)
    wall_full = lax.dynamic_update_slice_in_dim(
        jnp.zeros((chans, 9), jnp.float32), wall_part, first_chan, 0
    )
    class_full = lax.dynamic_update_slice_in_dim(
        jnp.zeros((classes, chans), jnp.float32), class_part, first_chan, 1
    )
    grad_widened = rim_tiles(grad_tile)
    grad_tile_vals = grad_tile.astype(jnp.float32)
    grad_field = jnp.zeros(features.shape, jnp.float32)
    tile_terms = []
    for i in range(5):
        for j in range(5):
            weight = tile_filter[:, 5 * i + j][:, None, None, None]
            grad_field = grad_field + weight * grad_widened[
                :, :, 4 - i : 4 - i + cells_x, 4 - j : 4 - j + cells_z
            ].astype(jnp.float32)
            shifted = widened[:, :, i : i + cells_x, j : j + cells_z].astype(jnp.float32)
            tile_terms.append(jnp.sum(shifted * grad_tile_vals, axis=(1, 2, 3)))
    tile_part = jnp.stack(tile_terms, axis=1)
    totals = lax.psum((tile_part, wall_full, class_full), ("gx", "gz", "col"))
    return (
        grad_field.astype(jnp.bfloat16),
        totals[0] / volume,
        totals[1] / volume,
        totals[2] / volume,
    )


def solution(mesh):
    return jax.shard_map(
        shards,
        mesh=mesh,
        in_specs=(
            P(None, "col", ("group", "gx"), "gz"),
            P(None, ("group", "gx"), "gz"),
            P(),
            P(),
            P(),
            P(),
            P(),
        ),
        out_specs=(
            P(None, "col", ("group", "gx"), "gz"),
            P("group", None),
            P("group", None),
            P("group", None),
        ),
        check_vma=False,
    )
```

profile of v0, /device:TPU:0, one launch (start us, length us, event | category | flops | bytes accessed | tf_op | source)
XLA Modules:
  0.0 227.5 jit_solution(17064217156550470900)
XLA Ops:
  7.2 1.1 copy.53
  8.4 3.1 %collective-permute-start = (bf16[32,32,2,128]{3,1,2,0:T(8,128)(2,1)S(1)}, bf16[32,32,2,128]{3,1,2,0:T(8,128)(2,1)S(1)}, u32[]{:S(2)}, u32[]{:S(2)}) collective-permute-start(bf16[32,32,2,128]{3,1,2,0:T(8,128)(2,1)S(1)} %copy.53), channel_id=1, source_target_pairs={{0,4},{4,8},{8,12},{12,0},{1,5},{5,9},{9,13},{13,1},{2,6},{6,10},{... | collective-permute-start | bytes 1572872 | tf_op jit(solution)/shard_map/ppermute | solution.py:14
  11.5 2.1 collective-permute-start.1
  13.6 0.8 fusion.110
  14.6 1.1 dynamic-slice_bitcast_fusion.8
  15.7 0.7 broadcast_multiply_fusion.4
  16.4 0.7 broadcast_multiply_fusion.2
  17.1 0.7 broadcast_multiply_fusion
  18.1 2.5 %slice_reduce_fusion.24 = (f32[32]{0:T(128)S(1)}, f32[32]{0:T(128)S(1)}, f32[32]{0:T(128)S(1)}, f32[32]{0:T(128)S(1)}, f32[32]{0:T(128)S(1)}, /*index=5*/f32[32]...) fusion(f32[32,25]{1,0:T(8,128)} %param.11), kind=kLoop, calls=%fused_computation.296 | loop fusion | bytes 4864 | tf_op jit(solution)/shard_map/slice | solution.py:117
  20.6 5.7 %collective-permute-done = bf16[32,32,2,128]{3,1,2,0:T(8,128)(2,1)S(1)} collective-permute-done((bf16[32,32,2,128]{3,1,2,0:T(8,128)(2,1)S(1)}, bf16[32,32,2,128]{3,1,2,0:T(8,128)(2,1)S(1)}, u32[]{:S(2)}, u32[]{:S(2)}) %collective-permute-start) | collective-permute-done | bytes 524320 | tf_op jit(solution)/shard_map/ppermute | solution.py:14
  26.3 1.4 constant_dynamic-update-slice_fusion.1
  27.7 8.4 %collective-permute-done.1 = bf16[32,32,2,128]{3,1,2,0:T(8,128)(2,1)S(1)} collective-permute-done((bf16[32,32,2,128]{3,1,2,0:T(8,128)(2,1)S(1)}, bf16[32,32,2,128]{3,1,2,0:T(8,128)(2,1)S(1)}, u32[]{:S(2)}, u32[]{:S(2)}) %collective-permute-start.1) | collective-permute-done | bytes 524320 | tf_op jit(solution)/shard_map/ppermute | solution.py:15
  36.1 0.8 copy-done.9
  37.0 1.9 fusion.129
  38.9 3.1 %copy.56 = bf16[32,32,6,2]{1,0,3,2:T(8,128)(2,1)} copy(bf16[32,32,6,2]{3,1,2,0:T(8,128)(2,1)} %get-tuple-element.96) | data formatting | bytes 49152 | tf_op jit(solution)/shard_map/slice | solution.py:12
  42.0 1.5 collective-permute-start.2
  43.5 2.1 copy.58
  46.2 0.8 slice_reduce_fusion.23
  47.0 2.2 copy.57
  49.2 1.4 collective-permute-done.3
  50.6 3.0 %copy.59 = bf16[32,32,6,2]{3,1,2,0:T(8,128)(2,1)} copy(bf16[32,32,6,2]{1,0,3,2:T(8,128)(2,1)} %collective-permute-done.3) | data formatting | bytes 49152 | tf_op jit(solution)/shard_map/ppermute | solution.py:15
  53.5 11.2 %fusion.90 = (bf16[32,32,2,128]{3,1,2,0:T(8,128)(2,1)S(1)}, bf16[32,32,2,128]{3,1,2,0:T(8,128)(2,1)}, bf16[32,32,2,128]{3,1,2,0:T(8,128)(2,1)}) fusion(bf16[32,32,2,128]{3,1,2,0:T(8,128)(2,1)} %copy-done.9, bf16[32,32,2,128]{3,1,2,0:T(8,128)(2,1)} %copy-done.5, bf16[32,32,2,128]{3,1,2,0:T(8,128)(2,1)} %copy-done.7, f32[32]{0:T(128)} %get-tuple-element.81, ...), kind=kLoop, calls=%fused_computation.211 | loop fusion | flops 37486592 | bytes 4770944 | tf_op jit(solution)/shard_map/convert_element_type | solution.py:65
  64.8 4.2 %all_to_all.36 = bf16[32,32,2,128]{3,1,2,0:T(8,128)(2,1)S(1)} all-to-all(bf16[32,32,2,128]{3,1,2,0:T(8,128)(2,1)S(1)} %get-tuple-element.88), channel_id=1, replica_groups=mesh['group'=2,'gx'=4,'gz'=2,'col'=2] {'col'}, dimensions={0} | all-to-all | bytes 1048576 | tf_op jit(solution)/shard_map/all_to_all | solution.py:71
  69.2 2.7 %fusion.88 = (f32[16,64,2,128]{3,0,2,1:T(8,128)S(1)}, f32[16,64,2,128]{3,0,2,1:T(8,128)}) fusion(f32[16,64]{0,1:T(8,128)S(1)} %get-tuple-element.138, f32[16,64]{0,1:T(8,128)S(1)} %get-tuple-element.140, f32[16,64]{0,1:T(8,128)S(1)} %get-tuple-element.134, f32[16,64]{0,1:T(8,128)S(1)} %get-tuple-element.142, bf16[16,64,2,128]{3,0,2,1:T(8,128)(2,1)S(1)} %bitcast.143, ...), kind=kLoop, calls=%fused_computation.209 | loop fusion | flops 7864320 | bytes 2658304 | tf_op jit(solution)/shard_map/mul | solution.py:77
  72.0 1.3 fusion.113
  73.4 18.9 %all-reduce.6.cloned.1.call-done = f32[4,64,2,128]{3,0,2,1:T(4,128)} async-done(((f32[4,64,2,128]{3,0,2,1:T(4,128)}), f32[4,64,2,128]{3,0,2,1:T(4,128)}) %all-reduce.6.cloned.1.call-update) | async-done | bytes 262160 | tf_op jit(solution)/shard_map/psum | solution.py:81
  92.3 4.8 %fusion.42 = (f32[16]{0:T(128)S(1)}, f32[16]{0:T(128)S(1)}, f32[16]{0:T(128)S(1)}, f32[16]{0:T(128)S(1)}, f32[16]{0:T(128)S(1)}, /*index=5*/f32[16]{0:T(128)S(1)...) fusion(f32[64]{0:T(128)} %copy-done.40, ...), kind=kOutput, calls=%fused_computation.162 | convolution fusion | flops 24838000 | bytes 2952516 | tf_op jit(solution)/shard_map/kc,kyxz->cyxz/dot_general | solution.py:86
  97.2 1.7 fusion.48
  99.0 4.3 %all_to_all.37 = bf16[16,64,2,128]{3,0,2,1:T(8,128)(2,1)S(1)} all-to-all(bf16[16,64,2,128]{3,0,2,1:T(8,128)(2,1)S(1)} %fusion.48), channel_id=1, replica_groups=mesh['group'=2,'gx'=4,'gz'=2,'col'=2] {'col'}, dimensions={1} | all-to-all | bytes 1048576 | tf_op jit(solution)/shard_map/all_to_all | solution.py:104
  103.5 3.9 %fusion.85 = (f32[32]{0:T(128)S(1)}, f32[32]{0:T(128)S(1)}, f32[32]{0:T(128)S(1)}, f32[32]{0:T(128)S(1)}, f32[32]{0:T(128)S(1)}, /*index=5*/f32[32]{0:T(128)S(1)}, f32[32]{0:T(128)S(1)}, f32[32]{0:T(128)S(1)}, f32[32]{0:T(128)S(1)}) fusion(bf16[2,16,32,2,128]{4,2,3,1,0:T(8,128)(2,1)S(1)} %copy.64, bf16[32,32,6,2]{3,1,2,0:T(8,128)(2,1)S(1)} %copy-done.3, ...), kind=kLoop, calls=%fused_computation.205 | loop fusion | flops 14417632 | bytes 2122880 | tf_op jit(solution)/shard_map/reduce_sum | solution.py:122
  107.5 3.8 %fusion.82 = (f32[32]{0:T(128)S(1)}, f32[32]{0:T(128)S(1)}, f32[32]{0:T(128)S(1)}, f32[32]{0:T(128)S(1)}, f32[32]{0:T(128)S(1)}, /*index=5*/f32[32]{0:T(128)S(1)}, f32[32]{0:T(128)S(1)}, f32[32]{0:T(128)S(1)}, f32[32]{0:T(128)S(1)}) fusion(bf16[2,16,32,2,128]{4,2,3,1,0:T(8,128)(2,1)S(1)} %copy.64, ...), kind=kLoop, calls=%fused_computation.202 | loop fusion | flops 14417632 | bytes 2122880 | tf_op jit(solution)/shard_map/reduce_sum | solution.py:122
  111.2 1.8 collective-permute-start.4
  113.0 2.1 collective-permute-start.5
  115.1 1.1 fusion.84
  116.2 1.4 convolution_bitcast_fusion
  118.2 72.8 %all-reduce.3 = (f32[32,25]{0,1:T(8,128)S(1)}, f32[32,9]{0,1:T(8,128)S(1)}, f32[4,32]{1,0:T(4,128)S(1)}) all-reduce(f32[32,25]{0,1:T(8,128)S(1)} %stack.133, f32[32,9]{0,1:T(8,128)S(1)} %dynamic_update_slice.6, f32[4,32]{1,0:T(4,128)S(1)} %dynamic_update_slice.7), channel_id=1, replica_groups=mesh['group'=2,'gx'=4,'gz'=2,'col'=2] {'gx','gz','col'}, use_global_device_ids=true, to_apply=%region_26.27 | all-reduce | flops 1216 | bytes 9728 | tf_op jit(solution)/shard_map/psum | solution.py:124
  191.6 0.8 copy-done.12
  192.4 1.4 pad_maximum_fusion.1
  193.7 2.4 %fusion.128 = (bf16[32,32,6,2]{3,1,2,0:T(8,128)(2,1)}, bf16[32,32,6,2]{3,1,2,0:T(8,128)(2,1)}) fusion(bf16[32,32,6,128]{3,1,2,0:T(8,128)(2,1)S(1)} %pad_maximum_fusion.1), kind=kLoop, calls=%fused_computation.344 | loop fusion | bytes 98304 | tf_op jit(solution)/shard_map/slice | solution.py:13
  196.2 2.6 %copy.75 = bf16[32,32,6,2]{1,0,3,2:T(8,128)(2,1)S(1)} copy(bf16[32,32,6,2]{3,1,2,0:T(8,128)(2,1)} %get-tuple-element.93) | data formatting | bytes 49152
  198.8 2.5 %copy.76 = bf16[32,32,6,2]{1,0,3,2:T(8,128)(2,1)S(1)} copy(bf16[32,32,6,2]{3,1,2,0:T(8,128)(2,1)} %get-tuple-element.94) | data formatting | bytes 49152
  201.4 2.1 collective-permute-start.7
  204.0 0.7 copy.72
  204.7 1.4 copy.66
  206.1 2.2 copy.68
  208.5 4.3 %pad_maximum_fusion = (bf16[32,32,6,130]{3,1,2,0:T(8,128)(2,1)S(1)}, bf16[32,32,6,130]{3,1,2,0:T(8,128)(2,1)S(1)}) fusion(bf16[32,32,6,2]{3,1,2,0:T(8,128)(2,1)S(1)} %copy.66, bf16[32,32,2,128]{3,1,2,0:T(8,128)(2,1)} %collective-permute-done.5, bf16[32,32,2,128]{3,1,2,0:T(8,128)(2,1)S(1)} %bitcast.139, bf16[32,32,2,128]{3,1,2,0:T(8,128)(2,1)S(1)} %copy-done.13, ...), kind=kLoop, calls=%fused_computation.72 | loop fusion | flops 12779520 | bytes 4816896 | tf_op jit(solution)/shard_map/concatenate | solution.py:16
  212.9 6.4 %fusion.89 = bf16[32,32,2,128]{3,1,2,0:T(8,128)(2,1)S(1)} fusion(bf16[32,32,2,128]{3,1,2,0:T(8,128)(2,1)S(1)} %copy-done.13, bf16[32,32,2,128]{3,1,2,0:T(8,128)(2,1)S(1)} %bitcast.140, bf16[32,32,2,128]{3,1,2,0:T(8,128)(2,1)} %collective-permute-done.5, bf16[32,32,6,130]{3,1,2,0:T(8,128)(2,1)S(1)} %get-tuple-element.92, ...), kind=kLoop, calls=%fused_computation.210 | loop fusion | flops 20185088 | bytes 12586112 | tf_op jit(solution)/shard_map/convert_element_type | solution.py:126
  219.3 1.3 copy.71
  (121 shorter events, 3.5 us)
Async XLA Ops:
  7.2 6.4 %copy-start = (f32[16,9]{1,0:T(8,128)S(1)}, f32[16,9]{1,0:T(8,128)}, u32[]{:S(2)}) copy-start(f32[16,9]{1,0:T(8,128)} %param.10) | copy-start | bytes 1732
  7.2 85.1 %all-reduce.6.cloned.1.call-start = ((), (), s32[]{:S(2)}) async-start(), calls=%async_computation.2 | async-start | bytes 524288 | tf_op jit(solution)/shard_map/psum | solution.py:81
  8.4 27.7 %copy-start.5 = (bf16[32,32,2,128]{3,1,2,0:T(8,128)(2,1)}, bf16[32,32,2,128]{3,1,2,0:T(8,128)(2,1)S(1)}, u32[]{:S(2)}) copy-start(bf16[32,32,2,128]{3,1,2,0:T(8,128)(2,1)S(1)} %copy.53) | copy-start | bytes 1572868
  8.4 17.9 %collective-permute-start = (bf16[32,32,2,128]{3,1,2,0:T(8,128)(2,1)S(1)}, bf16[32,32,2,128]{3,1,2,0:T(8,128)(2,1)S(1)}, u32[]{:S(2)}, u32[]{:S(2)}) collective-permute-start(bf16[32,32,2,128]{3,1,2,0:T(8,128)(2,1)S(1)} %copy.53), channel_id=1, source_target_pairs={{0,4},{4,8},{8,12},{12,0},{1,5},{5,9},{9,13},{13,1},{2,6},{6,10},{... | collective-permute-start | bytes 1572872 | tf_op jit(solution)/shard_map/ppermute | solution.py:14
  11.5 24.6 %collective-permute-start.1 = (bf16[32,32,2,128]{3,1,2,0:T(8,128)(2,1)S(1)}, bf16[32,32,2,128]{3,1,2,0:T(8,128)(2,1)S(1)}, u32[]{:S(2)}, u32[]{:S(2)}) collective-permute-start(bf16[32,32,2,128]{3,1,2,0:T(8,128)(2,1)S(1)} %copy.53), channel_id=1, source_target_pairs={{4,0},{8,4},{12,8},{0,12},{5,1},{9,5},{13,9},{1,13},{6,2},{10,6},{... | collective-permute-start | bytes 1572872 | tf_op jit(solution)/shard_map/ppermute | solution.py:15
  14.6 6.0 %copy-start.48 = (f32[64]{0:T(128)}, f32[64]{0:T(128)S(1)}, u32[]{:S(2)}) copy-start(f32[64]{0:T(128)S(1)} %get-tuple-element.113) | copy-start | bytes 772
  26.3 9.8 %copy-start.7 = (bf16[32,32,2,128]{3,1,2,0:T(8,128)(2,1)}, bf16[32,32,2,128]{3,1,2,0:T(8,128)(2,1)S(1)}, u32[]{:S(2)}) copy-start(bf16[32,32,2,128]{3,1,2,0:T(8,128)(2,1)S(1)} %collective-permute-done) | copy-start | bytes 1572868
  38.9 7.3 %copy-start.4 = (f32[32,25]{1,0:T(8,128)S(1)}, f32[32,25]{1,0:T(8,128)}, u32[]{:S(2)}) copy-start(f32[32,25]{1,0:T(8,128)} %param.11) | copy-start | bytes 9604
  42.0 5.0 %collective-permute-start.2 = (bf16[32,32,6,2]{1,0,3,2:T(8,128)(2,1)}, bf16[32,32,6,2]{1,0,3,2:T(8,128)(2,1)}, u32[]{:S(2)}, u32[]{:S(2)}) collective-permute-start(bf16[32,32,6,2]{1,0,3,2:T(8,128)(2,1)} %copy.56), channel_id=1, source_target_pairs={{0,2},{2,0},{1,3},{3,1},{4,6},{6,4},{5,7},{7,5},{8,10},{10,8},{9,1... | collective-permute-start | bytes 73736 | tf_op jit(solution)/shard_map/ppermute | solution.py:14
  45.6 4.9 %collective-permute-start.3 = (bf16[32,32,6,2]{1,0,3,2:T(8,128)(2,1)}, bf16[32,32,6,2]{1,0,3,2:T(8,128)(2,1)}, u32[]{:S(2)}, u32[]{:S(2)}) collective-permute-start(bf16[32,32,6,2]{1,0,3,2:T(8,128)(2,1)} %copy.58), channel_id=1, source_target_pairs={{2,0},{0,2},{3,1},{1,3},{6,4},{4,6},{7,5},{5,7},{10,8},{8,10},{11,... | collective-permute-start | bytes 73736 | tf_op jit(solution)/shard_map/ppermute | solution.py:15
  49.2 15.6 %copy-start.1 = (bf16[32,32,6,2]{3,1,2,0:T(8,128)(2,1)}, bf16[32,32,6,2]{3,1,2,0:T(8,128)(2,1)S(1)}, u32[]{:S(2)}) copy-start(bf16[32,32,6,2]{3,1,2,0:T(8,128)(2,1)S(1)} %copy.57) | copy-start | bytes 73732
  64.7 7.2 %copy-start.39 = (f32[4,32]{1,0:T(4,128)S(1)}, f32[4,32]{1,0:T(4,128)}, u32[]{:S(2)}) copy-start(f32[4,32]{1,0:T(4,128)} %param.13) | copy-start | bytes 1540
  92.3 4.9 %copy-start.17 = (f32[16,64]{0,1:T(8,128)S(1)}, f32[16,64]{0,1:T(8,128)}, u32[]{:S(2)}) copy-start(f32[16,64]{0,1:T(8,128)} %get-tuple-element.129) | copy-start | bytes 12292
  92.3 4.9 %copy-start.18 = (f32[16,64]{0,1:T(8,128)S(1)}, f32[16,64]{0,1:T(8,128)}, u32[]{:S(2)}) copy-start(f32[16,64]{0,1:T(8,128)} %get-tuple-element.145) | copy-start | bytes 12292
  92.3 4.9 %copy-start.19 = (f32[16,64]{0,1:T(8,128)S(1)}, f32[16,64]{0,1:T(8,128)}, u32[]{:S(2)}) copy-start(f32[16,64]{0,1:T(8,128)} %get-tuple-element.133) | copy-start | bytes 12292
  92.3 4.9 %copy-start.20 = (f32[16,64]{0,1:T(8,128)S(1)}, f32[16,64]{0,1:T(8,128)}, u32[]{:S(2)}) copy-start(f32[16,64]{0,1:T(8,128)} %get-tuple-element.143) | copy-start | bytes 12292
  92.3 4.9 %copy-start.21 = (f32[16,64]{0,1:T(8,128)S(1)}, f32[16,64]{0,1:T(8,128)}, u32[]{:S(2)}) copy-start(f32[16,64]{0,1:T(8,128)} %get-tuple-element.137) | copy-start | bytes 12292
  92.3 4.9 %copy-start.22 = (f32[16,64]{0,1:T(8,128)S(1)}, f32[16,64]{0,1:T(8,128)}, u32[]{:S(2)}) copy-start(f32[16,64]{0,1:T(8,128)} %get-tuple-element.141) | copy-start | bytes 12292
  97.1 6.3 %copy-start.3 = (bf16[32,32,6,2]{3,1,2,0:T(8,128)(2,1)S(1)}, bf16[32,32,6,2]{3,1,2,0:T(8,128)(2,1)}, u32[]{:S(2)}) copy-start(bf16[32,32,6,2]{3,1,2,0:T(8,128)(2,1)} %copy.59) | copy-start | bytes 73732
  98.9 8.5 %copy-start.2 = (bf16[32,32,6,2]{3,1,2,0:T(8,128)(2,1)S(1)}, bf16[32,32,6,2]{3,1,2,0:T(8,128)(2,1)}, u32[]{:S(2)}) copy-start(bf16[32,32,6,2]{3,1,2,0:T(8,128)(2,1)} %copy-done.1) | copy-start | bytes 73732
  103.5 11.6 %copy-start.6 = (bf16[32,32,2,128]{3,1,2,0:T(8,128)(2,1)S(1)}, bf16[32,32,2,128]{3,1,2,0:T(8,128)(2,1)}, u32[]{:S(2)}) copy-start(bf16[32,32,2,128]{3,1,2,0:T(8,128)(2,1)} %copy-done.5) | copy-start | bytes 1572868
  103.5 11.6 %copy-start.8 = (bf16[32,32,2,128]{3,1,2,0:T(8,128)(2,1)S(1)}, bf16[32,32,2,128]{3,1,2,0:T(8,128)(2,1)}, u32[]{:S(2)}) copy-start(bf16[32,32,2,128]{3,1,2,0:T(8,128)(2,1)} %copy-done.7) | copy-start | bytes 1572868
  103.5 11.6 %copy-start.10 = (bf16[32,32,2,128]{3,1,2,0:T(8,128)(2,1)S(1)}, bf16[32,32,2,128]{3,1,2,0:T(8,128)(2,1)}, u32[]{:S(2)}) copy-start(bf16[32,32,2,128]{3,1,2,0:T(8,128)(2,1)} %copy-done.9) | copy-start | bytes 1572868
  103.5 11.6 %copy-start.11 = (bf16[32,32,2,128]{3,2,1,0:T(2,128)(2,1)S(1)}, bf16[32,32,2,128]{3,2,1,0:T(2,128)(2,1)}, u32[]{:S(2)}) copy-start(bf16[32,32,2,128]{3,2,1,0:T(2,128)(2,1)} %param.7) | copy-start | bytes 1572868
  103.5 11.6 %copy-start.14 = (bf16[32,32,2,128]{3,1,2,0:T(8,128)(2,1)S(1)}, bf16[32,32,2,128]{3,1,2,0:T(8,128)(2,1)}, u32[]{:S(2)}) copy-start(bf16[32,32,2,128]{3,1,2,0:T(8,128)(2,1)} %get-tuple-element.89) | copy-start | bytes 1572868
  103.5 11.6 %copy-start.15 = (bf16[32,32,2,128]{3,1,2,0:T(8,128)(2,1)S(1)}, bf16[32,32,2,128]{3,1,2,0:T(8,128)(2,1)}, u32[]{:S(2)}) copy-start(bf16[32,32,2,128]{3,1,2,0:T(8,128)(2,1)} %get-tuple-element.90) | copy-start | bytes 1572868
  107.4 8.8 %copy-start.16 = (f32[4,64,2,128]{3,0,2,1:T(4,128)S(1)}, f32[4,64,2,128]{3,0,2,1:T(4,128)}, u32[]{:S(2)}) copy-start(f32[4,64,2,128]{3,0,2,1:T(4,128)} %all-reduce.6.cloned.1.call-done) | copy-start | bytes 786436
  107.4 8.8 %copy-start.23 = (s32[64,2,128]{2,1,0:T(2,128)S(1)}, s32[64,2,128]{2,1,0:T(2,128)}, u32[]{:S(2)}) copy-start(s32[64,2,128]{2,1,0:T(2,128)} %param.8) | copy-start | bytes 196612
  111.2 80.3 %collective-permute-start.4 = (bf16[32,32,2,128]{3,1,2,0:T(8,128)(2,1)S(1)}, bf16[32,32,2,128]{3,1,2,0:T(8,128)(2,1)S(1)}, u32[]{:S(2)}, u32[]{:S(2)}) collective-permute-start(bf16[32,32,2,128]{3,1,2,0:T(8,128)(2,1)S(1)} %bitcast.136), channel_id=1, source_target_pairs={{0,4},{4,8},{8,12},{12,0},{1,5},{5,9},{9,13},{13,1},{2,6},{6,10},{... | collective-permute-start | bytes 1572872 | tf_op jit(solution)/shard_map/ppermute | solution.py:14
  113.0 79.4 %collective-permute-start.5 = (bf16[32,32,2,128]{3,1,2,0:T(8,128)(2,1)S(1)}, bf16[32,32,2,128]{3,1,2,0:T(8,128)(2,1)}, u32[]{:S(2)}, u32[]{:S(2)}) collective-permute-start(bf16[32,32,2,128]{3,1,2,0:T(8,128)(2,1)S(1)} %bitcast.137), channel_id=1, source_target_pairs={{4,0},{8,4},{12,8},{0,12},{5,1},{9,5},{13,9},{1,13},{6,2},{10,6},{... | collective-permute-start | bytes 1572872 | tf_op jit(solution)/shard_map/ppermute | solution.py:15
  196.2 12.2 %copy-start.13 = (bf16[32,32,2,128]{3,1,2,0:T(8,128)(2,1)S(1)}, bf16[32,32,2,128]{3,1,2,0:T(8,128)(2,1)}, u32[]{:S(2)}) copy-start(bf16[32,32,2,128]{3,1,2,0:T(8,128)(2,1)} %copy-done.12) | copy-start | bytes 1572868
  198.8 6.0 %collective-permute-start.6 = (bf16[32,32,6,2]{1,0,3,2:T(8,128)(2,1)S(1)}, bf16[32,32,6,2]{1,0,3,2:T(8,128)(2,1)S(1)}, u32[]{:S(2)}, u32[]{:S(2)}) collective-permute-start(bf16[32,32,6,2]{1,0,3,2:T(8,128)(2,1)S(1)} %copy.75), channel_id=1, source_target_pairs={{2,0},{0,2},{3,1},{1,3},{6,4},{4,6},{7,5},{5,7},{10,8},{8,10},{11,... | collective-permute-start | bytes 73736 | tf_op jit(solution)/shard_map/ppermute | solution.py:15
  201.4 4.7 %collective-permute-start.7 = (bf16[32,32,6,2]{1,0,3,2:T(8,128)(2,1)S(1)}, bf16[32,32,6,2]{1,0,3,2:T(8,128)(2,1)S(1)}, u32[]{:S(2)}, u32[]{:S(2)}) collective-permute-start(bf16[32,32,6,2]{1,0,3,2:T(8,128)(2,1)S(1)} %copy.76), channel_id=1, source_target_pairs={{0,2},{2,0},{1,3},{3,1},{4,6},{6,4},{5,7},{7,5},{8,10},{10,8},{9,1... | collective-permute-start | bytes 73736 | tf_op jit(solution)/shard_map/ppermute | solution.py:14
  208.3 4.4 %copy-start.24 = (f32[32]{0:T(128)S(1)}, f32[32]{0:T(128)}, u32[]{:S(2)}) copy-start(f32[32]{0:T(128)} %get-tuple-element.64) | copy-start | bytes 388
  208.3 4.4 %copy-start.25 = (f32[32]{0:T(128)S(1)}, f32[32]{0:T(128)}, u32[]{:S(2)}) copy-start(f32[32]{0:T(128)} %get-tuple-element.65) | copy-start | bytes 388
  208.3 4.4 %copy-start.26 = (f32[32]{0:T(128)S(1)}, f32[32]{0:T(128)}, u32[]{:S(2)}) copy-start(f32[32]{0:T(128)} %get-tuple-element.66) | copy-start | bytes 388
  208.3 4.4 %copy-start.27 = (f32[32]{0:T(128)S(1)}, f32[32]{0:T(128)}, u32[]{:S(2)}) copy-start(f32[32]{0:T(128)} %get-tuple-element.67) | copy-start | bytes 388
  208.4 4.4 %copy-start.28 = (f32[32]{0:T(128)S(1)}, f32[32]{0:T(128)}, u32[]{:S(2)}) copy-start(f32[32]{0:T(128)} %get-tuple-element.68) | copy-start | bytes 388
  208.4 4.4 %copy-start.29 = (f32[32]{0:T(128)S(1)}, f32[32]{0:T(128)}, u32[]{:S(2)}) copy-start(f32[32]{0:T(128)} %get-tuple-element.69) | copy-start | bytes 388
  208.4 4.4 %copy-start.30 = (f32[32]{0:T(128)S(1)}, f32[32]{0:T(128)}, u32[]{:S(2)}) copy-start(f32[32]{0:T(128)} %get-tuple-element.70) | copy-start | bytes 388
  208.4 4.4 %copy-start.31 = (f32[32]{0:T(128)S(1)}, f32[32]{0:T(128)}, u32[]{:S(2)}) copy-start(f32[32]{0:T(128)} %get-tuple-element.71) | copy-start | bytes 388
  208.4 4.4 %copy-start.32 = (f32[32]{0:T(128)S(1)}, f32[32]{0:T(128)}, u32[]{:S(2)}) copy-start(f32[32]{0:T(128)} %get-tuple-element.72) | copy-start | bytes 388
  208.4 4.4 %copy-start.33 = (f32[32]{0:T(128)S(1)}, f32[32]{0:T(128)}, u32[]{:S(2)}) copy-start(f32[32]{0:T(128)} %get-tuple-element.73) | copy-start | bytes 388
  208.4 4.4 %copy-start.34 = (f32[32]{0:T(128)S(1)}, f32[32]{0:T(128)}, u32[]{:S(2)}) copy-start(f32[32]{0:T(128)} %get-tuple-element.74) | copy-start | bytes 388
  208.4 4.4 %copy-start.35 = (f32[32]{0:T(128)S(1)}, f32[32]{0:T(128)}, u32[]{:S(2)}) copy-start(f32[32]{0:T(128)} %get-tuple-element.75) | copy-start | bytes 388
  208.4 4.4 %copy-start.36 = (f32[32]{0:T(128)S(1)}, f32[32]{0:T(128)}, u32[]{:S(2)}) copy-start(f32[32]{0:T(128)} %get-tuple-element.76) | copy-start | bytes 388
  208.4 4.4 %copy-start.37 = (f32[32]{0:T(128)S(1)}, f32[32]{0:T(128)}, u32[]{:S(2)}) copy-start(f32[32]{0:T(128)} %get-tuple-element.81) | copy-start | bytes 388
  208.5 4.4 %copy-start.38 = (f32[32]{0:T(128)S(1)}, f32[32]{0:T(128)}, u32[]{:S(2)}) copy-start(f32[32]{0:T(128)} %get-tuple-element.82) | copy-start | bytes 388
  (10 other events, 28.0 us)
Sparse Core Ops, SparseCore 0:
  73.5 18.7 all-reduce.5
where the time goes:
time: 228 us; the launch traced here: 227 us
  blocking collectives  81.2 us (36%)
  other arithmetic  39.9 us (18%)
  local copies, waits for them, and re-layouts  35.5 us (16%)
  waiting for transfers between devices  34.4 us (15%)
  between operations  14.8 us (6%)
  starting transfers between devices  13.2 us (6%)
  matrix products  8.43 us (4%)
    psum x1, blocking collectives, shards(): totals = lax.psum((tile_part, wall_full, class_full), ('gx', 'gz', 'col'))  72.8 us
    psum x1, waiting for transfers between devices, shards(): scores = lax.psum(partial_scores, 'col')  18.9 us
    unnamed x105, local copies, waits for them, and re-layouts  11.5 us
    convert_element_type x1, other arithmetic, shards(): smoothed = smooth.astype(jnp.bfloat16)  11.2 us
    ppermute x4, waiting for transfers between devices, with_halo(): after = lax.ppermute(leading, axis, down)  9.77 us
    reduce_sum x3, other arithmetic, shards(): tile_terms.append(jnp.sum(shifted * grad_tile_vals, axis=(1, 2, 3)))  8.73 us
    ppermute x4, starting transfers between devices, with_halo(): before = lax.ppermute(last, axis, up)  8.43 us
    slice x3, local copies, waits for them, and re-layouts, with_halo(): leading = lax.slice_in_dim(value, 0, width, axis=dim)  6.44 us
  transfers between devices with their start and end apart: 9, of which 4 were waited for; matrix products, arithmetic and copies ran while one was open for 10% of the time, Pallas kernels for 0%

commit v1 on v0

--- a/solution.py
+++ b/solution.py
@@ -121,7 +121,9 @@
             shifted = widened[:, :, i : i + cells_x, j : j + cells_z].astype(jnp.float32)
             tile_terms.append(jnp.sum(shifted * grad_tile_vals, axis=(1, 2, 3)))
     tile_part = jnp.stack(tile_terms, axis=1)
-    totals = lax.psum((tile_part, wall_full, class_full), ("gx", "gz", "col"))
+    totals = (tile_part, wall_full, class_full)
+    for mesh_axis in (("gz", "col"), "gx"):
+        totals = lax.psum(totals, mesh_axis)
     return (
         grad_field.astype(jnp.bfloat16),
         totals[0] / volume,

time: 228 us -> 188 us (0.82)
  blocking collectives: 81.2 us -> 39.6 us
    psum x1 -> x2, blocking collectives: 72.8 us -> 31.2 us  [shards(): totals = lax.psum(totals, mesh_axis)]
  transfers between devices with their start and end apart: 9 -> 9, of which waited for: 4 -> 5; matrix products, arithmetic and copies ran while one was open for 10% -> 12% of each run, Pallas kernels for 0% -> 0%
where the time goes in v1:
time: 188 us; the launch traced here: 187 us
  other arithmetic  39.9 us (21%)
  blocking collectives  39.6 us (21%)
  waiting for transfers between devices  35.7 us (19%)
  local copies, waits for them, and re-layouts  35.5 us (19%)
  between operations  14.7 us (8%)
  starting transfers between devices  13.3 us (7%)
  matrix products  8.43 us (4%)
    psum x2, blocking collectives, shards(): totals = lax.psum(totals, mesh_axis)  31.2 us
    psum x1, waiting for transfers between devices, shards(): scores = lax.psum(partial_scores, 'col')  18.9 us
    unnamed x105, local copies, waits for them, and re-layouts  11.5 us
    convert_element_type x1, other arithmetic, shards(): smoothed = smooth.astype(jnp.bfloat16)  11.2 us
    ppermute x4, waiting for transfers between devices, with_halo(): after = lax.ppermute(leading, axis, down)  9.77 us
    reduce_sum x3, other arithmetic, shards(): tile_terms.append(jnp.sum(shifted * grad_tile_vals, axis=(1, 2, 3)))  8.73 us
    ppermute x4, starting transfers between devices, with_halo(): before = lax.ppermute(last, axis, up)  7.05 us
    ppermute x4, waiting for transfers between devices, with_halo(): before = lax.ppermute(last, axis, up)  7.04 us
  transfers between devices with their start and end apart: 9, of which 5 were waited for; matrix products, arithmetic and copies ran while one was open for 12% of the time, Pallas kernels for 0%

profile of v1, /device:TPU:0, one launch (start us, length us, event | category | flops | bytes accessed | tf_op | source)
XLA Modules:
  0.0 187.2 jit_solution(7558691039119144272)
XLA Ops:
  7.2 1.1 copy.53
  8.4 3.1 %collective-permute-start = (bf16[32,32,2,128]{3,1,2,0:T(8,128)(2,1)S(1)}, bf16[32,32,2,128]{3,1,2,0:T(8,128)(2,1)S(1)}, u32[]{:S(2)}, u32[]{:S(2)}) collective-permute-start(bf16[32,32,2,128]{3,1,2,0:T(8,128)(2,1)S(1)} %copy.53), channel_id=1, source_target_pairs={{0,4},{4,8},{8,12},{12,0},{1,5},{5,9},{9,13},{13,1},{2,6},{6,10},{... | collective-permute-start | bytes 1572872 | tf_op jit(solution)/shard_map/ppermute | solution.py:14
  11.5 2.1 %collective-permute-start.1 = (bf16[32,32,2,128]{3,1,2,0:T(8,128)(2,1)S(1)}, bf16[32,32,2,128]{3,1,2,0:T(8,128)(2,1)S(1)}, u32[]{:S(2)}, u32[]{:S(2)}) collective-permute-start(bf16[32,32,2,128]{3,1,2,0:T(8,128)(2,1)S(1)} %copy.53), channel_id=1, source_target_pairs={{4,0},{8,4},{12,8},{0,12},{5,1},{9,5},{13,9},{1,13},{6,2},{10,6},{... | collective-permute-start | bytes 1572872 | tf_op jit(solution)/shard_map/ppermute | solution.py:15
  13.6 0.8 fusion.110
  14.6 1.1 dynamic-slice_bitcast_fusion.8
  15.7 0.7 broadcast_multiply_fusion.4
  16.4 0.7 broadcast_multiply_fusion.2
  18.1 2.5 %slice_reduce_fusion.24 = (f32[32]{0:T(128)S(1)}, f32[32]{0:T(128)S(1)}, f32[32]{0:T(128)S(1)}, f32[32]{0:T(128)S(1)}, f32[32]{0:T(128)S(1)}, /*index=5*/f32[32]...) fusion(f32[32,25]{1,0:T(8,128)} %param.11), kind=kLoop, calls=%fused_computation.296 | loop fusion | bytes 4864 | tf_op jit(solution)/shard_map/slice | solution.py:117
  20.6 5.7 %collective-permute-done = bf16[32,32,2,128]{3,1,2,0:T(8,128)(2,1)S(1)} collective-permute-done((bf16[32,32,2,128]{3,1,2,0:T(8,128)(2,1)S(1)}, bf16[32,32,2,128]{3,1,2,0:T(8,128)(2,1)S(1)}, u32[]{:S(2)}, u32[]{:S(2)}) %collective-permute-start) | collective-permute-done | bytes 524320 | tf_op jit(solution)/shard_map/ppermute | solution.py:14
  26.3 1.4 constant_dynamic-update-slice_fusion.1
  27.7 8.4 %collective-permute-done.1 = bf16[32,32,2,128]{3,1,2,0:T(8,128)(2,1)S(1)} collective-permute-done((bf16[32,32,2,128]{3,1,2,0:T(8,128)(2,1)S(1)}, bf16[32,32,2,128]{3,1,2,0:T(8,128)(2,1)S(1)}, u32[]{:S(2)}, u32[]{:S(2)}) %collective-permute-start.1) | collective-permute-done | bytes 524320 | tf_op jit(solution)/shard_map/ppermute | solution.py:15
  36.1 0.8 copy-done.9
  37.0 1.9 %fusion.129 = (bf16[32,32,6,2]{3,1,2,0:T(8,128)(2,1)S(1)}, bf16[32,32,6,2]{3,1,2,0:T(8,128)(2,1)}) fusion(bf16[32,32,6,128]{3,1,2,0:T(8,128)(2,1)S(1)} %constant_dynamic-update-slice_fusion), kind=kLoop, calls=%fused_computation.345 | loop fusion | bytes 98304 | tf_op jit(solution)/shard_map/slice | solution.py:13
  38.9 3.1 %copy.56 = bf16[32,32,6,2]{1,0,3,2:T(8,128)(2,1)} copy(bf16[32,32,6,2]{3,1,2,0:T(8,128)(2,1)} %get-tuple-element.99) | data formatting | bytes 49152 | tf_op jit(solution)/shard_map/slice | solution.py:12
  42.0 1.5 collective-permute-start.2
  43.5 2.1 %copy.58 = bf16[32,32,6,2]{1,0,3,2:T(8,128)(2,1)} copy(bf16[32,32,6,2]{3,1,2,0:T(8,128)(2,1)S(1)} %get-tuple-element.98) | data formatting | bytes 49152 | tf_op jit(solution)/shard_map/slice | solution.py:13
  46.2 0.8 slice_reduce_fusion.23
  47.0 2.2 %copy.57 = bf16[32,32,6,2]{3,1,2,0:T(8,128)(2,1)S(1)} copy(bf16[32,32,6,2]{1,0,3,2:T(8,128)(2,1)} %collective-permute-done.2) | data formatting | bytes 49152 | tf_op jit(solution)/shard_map/ppermute | solution.py:14
  49.2 1.4 collective-permute-done.3
  50.6 3.0 %copy.59 = bf16[32,32,6,2]{3,1,2,0:T(8,128)(2,1)} copy(bf16[32,32,6,2]{1,0,3,2:T(8,128)(2,1)} %collective-permute-done.3) | data formatting | bytes 49152 | tf_op jit(solution)/shard_map/ppermute | solution.py:15
  53.5 11.2 %fusion.90 = (bf16[32,32,2,128]{3,1,2,0:T(8,128)(2,1)S(1)}, bf16[32,32,2,128]{3,1,2,0:T(8,128)(2,1)}, bf16[32,32,2,128]{3,1,2,0:T(8,128)(2,1)}) fusion(bf16[32,32,2,128]{3,1,2,0:T(8,128)(2,1)} %copy-done.9, bf16[32,32,2,128]{3,1,2,0:T(8,128)(2,1)} %copy-done.5, bf16[32,32,2,128]{3,1,2,0:T(8,128)(2,1)} %copy-done.7, f32[32]{0:T(128)} %get-tuple-element.81, ...), kind=kLoop, calls=%fused_computation.211 | loop fusion | flops 37486592 | bytes 4770944 | tf_op jit(solution)/shard_map/convert_element_type | solution.py:65
  64.8 4.2 %all_to_all.36 = bf16[32,32,2,128]{3,1,2,0:T(8,128)(2,1)S(1)} all-to-all(bf16[32,32,2,128]{3,1,2,0:T(8,128)(2,1)S(1)} %get-tuple-element.91), channel_id=1, replica_groups=mesh['group'=2,'gx'=4,'gz'=2,'col'=2] {'col'}, dimensions={0} | all-to-all | bytes 1048576 | tf_op jit(solution)/shard_map/all_to_all | solution.py:71
  69.2 2.7 %fusion.88 = (f32[16,64,2,128]{3,0,2,1:T(8,128)S(1)}, f32[16,64,2,128]{3,0,2,1:T(8,128)}) fusion(f32[16,64]{0,1:T(8,128)S(1)} %get-tuple-element.141, f32[16,64]{0,1:T(8,128)S(1)} %get-tuple-element.143, f32[16,64]{0,1:T(8,128)S(1)} %get-tuple-element.137, f32[16,64]{0,1:T(8,128)S(1)} %get-tuple-element.145, bf16[16,64,2,128]{3,0,2,1:T(8,128)(2,1)S(1)} %bitcast.143, ...), kind=kLoop, calls=%fused_computation.209 | loop fusion | flops 7864320 | bytes 2658304 | tf_op jit(solution)/shard_map/mul | solution.py:77
  72.0 1.3 fusion.113
  73.4 18.9 %all-reduce.7.cloned.1.call-done = f32[4,64,2,128]{3,0,2,1:T(4,128)} async-done(((f32[4,64,2,128]{3,0,2,1:T(4,128)}), f32[4,64,2,128]{3,0,2,1:T(4,128)}) %all-reduce.7.cloned.1.call-update) | async-done | bytes 262160 | tf_op jit(solution)/shard_map/psum | solution.py:81
  92.3 4.8 %fusion.42 = (f32[16]{0:T(128)S(1)}, f32[16]{0:T(128)S(1)}, f32[16]{0:T(128)S(1)}, f32[16]{0:T(128)S(1)}, f32[16]{0:T(128)S(1)}, /*index=5*/f32[16]{0:T(128)S(1)...) fusion(f32[64]{0:T(128)} %copy-done.40, ...), kind=kOutput, calls=%fused_computation.162 | convolution fusion | flops 24838000 | bytes 2952516 | tf_op jit(solution)/shard_map/kc,kyxz->cyxz/dot_general | solution.py:86
  97.2 1.7 fusion.48
  99.0 4.3 %all_to_all.37 = bf16[16,64,2,128]{3,0,2,1:T(8,128)(2,1)S(1)} all-to-all(bf16[16,64,2,128]{3,0,2,1:T(8,128)(2,1)S(1)} %fusion.48), channel_id=1, replica_groups=mesh['group'=2,'gx'=4,'gz'=2,'col'=2] {'col'}, dimensions={1} | all-to-all | bytes 1048576 | tf_op jit(solution)/shard_map/all_to_all | solution.py:104
  103.5 3.9 %fusion.85 = (f32[32]{0:T(128)S(1)}, f32[32]{0:T(128)S(1)}, f32[32]{0:T(128)S(1)}, f32[32]{0:T(128)S(1)}, f32[32]{0:T(128)S(1)}, /*index=5*/f32[32]{0:T(128)S(1)}, f32[32]{0:T(128)S(1)}, f32[32]{0:T(128)S(1)}, f32[32]{0:T(128)S(1)}) fusion(bf16[2,16,32,2,128]{4,2,3,1,0:T(8,128)(2,1)S(1)} %copy.64, bf16[32,32,6,2]{3,1,2,0:T(8,128)(2,1)S(1)} %copy-done.3, ...), kind=kLoop, calls=%fused_computation.205 | loop fusion | flops 14417632 | bytes 2122880 | tf_op jit(solution)/shard_map/reduce_sum | solution.py:122
  107.5 3.8 %fusion.82 = (f32[32]{0:T(128)S(1)}, f32[32]{0:T(128)S(1)}, f32[32]{0:T(128)S(1)}, f32[32]{0:T(128)S(1)}, f32[32]{0:T(128)S(1)}, /*index=5*/f32[32]{0:T(128)S(1)}, f32[32]{0:T(128)S(1)}, f32[32]{0:T(128)S(1)}, f32[32]{0:T(128)S(1)}) fusion(bf16[2,16,32,2,128]{4,2,3,1,0:T(8,128)(2,1)S(1)} %copy.64, ...), kind=kLoop, calls=%fused_computation.202 | loop fusion | flops 14417632 | bytes 2122880 | tf_op jit(solution)/shard_map/reduce_sum | solution.py:122
  111.2 1.8 collective-permute-start.4
  113.0 2.1 %collective-permute-start.5 = (bf16[32,32,2,128]{3,1,2,0:T(8,128)(2,1)S(1)}, bf16[32,32,2,128]{3,1,2,0:T(8,128)(2,1)}, u32[]{:S(2)}, u32[]{:S(2)}) collective-permute-start(bf16[32,32,2,128]{3,1,2,0:T(8,128)(2,1)S(1)} %bitcast.137), channel_id=1, source_target_pairs={{4,0},{8,4},{12,8},{0,12},{5,1},{9,5},{13,9},{1,13},{6,2},{10,6},{... | collective-permute-start | bytes 1572872 | tf_op jit(solution)/shard_map/ppermute | solution.py:15
  115.1 1.1 fusion.84
  116.2 1.4 convolution_bitcast_fusion
  118.2 12.1 %all-reduce.3 = (f32[32,25]{0,1:T(8,128)S(1)}, f32[32,9]{0,1:T(8,128)S(1)}, f32[4,32]{1,0:T(4,128)S(1)}) all-reduce(f32[32,25]{0,1:T(8,128)S(1)} %stack.133, f32[32,9]{0,1:T(8,128)S(1)} %dynamic_update_slice.6, f32[4,32]{1,0:T(4,128)S(1)} %dynamic_update_slice.7), channel_id=1, replica_groups=mesh['group'=2,'gx'=4,'gz'=2,'col'=2] {'gz','col'}, use_global_device_ids=true, to_apply=%region_26.27 | all-reduce | flops 1216 | bytes 9728 | tf_op jit(solution)/shard_map/psum | solution.py:126
  130.2 19.1 %all-reduce.4 = (f32[32,25]{0,1:T(8,128)S(1)}, f32[32,9]{0,1:T(8,128)S(1)}, f32[4,32]{1,0:T(4,128)S(1)}) all-reduce(f32[32,25]{0,1:T(8,128)S(1)} %get-tuple-element.83, f32[32,9]{0,1:T(8,128)S(1)} %get-tuple-element.84, f32[4,32]{1,0:T(4,128)S(1)} %get-tuple-element.85), channel_id=1, replica_groups=mesh['group'=2,'gx'=4,'gz'=2,'col'=2] {'gx'}, use_global_device_ids=true, to_apply=%region_27.28 | all-reduce | flops 1216 | bytes 9728 | tf_op jit(solution)/shard_map/psum | solution.py:126
  149.9 0.8 copy-done.12
  150.7 1.4 pad_maximum_fusion.1
  152.1 2.4 %fusion.128 = (bf16[32,32,6,2]{3,1,2,0:T(8,128)(2,1)}, bf16[32,32,6,2]{3,1,2,0:T(8,128)(2,1)}) fusion(bf16[32,32,6,128]{3,1,2,0:T(8,128)(2,1)S(1)} %pad_maximum_fusion.1), kind=kLoop, calls=%fused_computation.344 | loop fusion | bytes 98304 | tf_op jit(solution)/shard_map/slice | solution.py:13
  154.5 2.6 %copy.75 = bf16[32,32,6,2]{1,0,3,2:T(8,128)(2,1)S(1)} copy(bf16[32,32,6,2]{3,1,2,0:T(8,128)(2,1)} %get-tuple-element.96) | data formatting | bytes 49152
  157.1 1.5 collective-permute-start.6
  158.6 2.5 %copy.76 = bf16[32,32,6,2]{1,0,3,2:T(8,128)(2,1)S(1)} copy(bf16[32,32,6,2]{3,1,2,0:T(8,128)(2,1)} %get-tuple-element.97) | data formatting | bytes 49152
  163.1 1.4 copy.66
  164.5 1.3 collective-permute-done.7
  165.8 2.2 %copy.68 = bf16[32,32,6,2]{3,1,2,0:T(8,128)(2,1)} copy(bf16[32,32,6,2]{1,0,3,2:T(8,128)(2,1)S(1)} %collective-permute-done.7) | data formatting | bytes 49152 | tf_op jit(solution)/shard_map/ppermute | solution.py:14
  168.2 4.3 %pad_maximum_fusion = (bf16[32,32,6,130]{3,1,2,0:T(8,128)(2,1)S(1)}, bf16[32,32,6,130]{3,1,2,0:T(8,128)(2,1)S(1)}) fusion(bf16[32,32,6,2]{3,1,2,0:T(8,128)(2,1)S(1)} %copy.66, bf16[32,32,2,128]{3,1,2,0:T(8,128)(2,1)} %collective-permute-done.5, bf16[32,32,2,128]{3,1,2,0:T(8,128)(2,1)S(1)} %bitcast.139, bf16[32,32,2,128]{3,1,2,0:T(8,128)(2,1)S(1)} %copy-done.13, ...), kind=kLoop, calls=%fused_computation.72 | loop fusion | flops 12779520 | bytes 4816896 | tf_op jit(solution)/shard_map/concatenate | solution.py:16
  172.6 6.4 %fusion.89 = bf16[32,32,2,128]{3,1,2,0:T(8,128)(2,1)S(1)} fusion(bf16[32,32,2,128]{3,1,2,0:T(8,128)(2,1)S(1)} %copy-done.13, bf16[32,32,2,128]{3,1,2,0:T(8,128)(2,1)S(1)} %bitcast.140, bf16[32,32,2,128]{3,1,2,0:T(8,128)(2,1)} %collective-permute-done.5, bf16[32,32,6,130]{3,1,2,0:T(8,128)(2,1)S(1)} %get-tuple-element.95, ...), kind=kLoop, calls=%fused_computation.210 | loop fusion | flops 20185088 | bytes 12586112 | tf_op jit(solution)/shard_map/convert_element_type | solution.py:128
  179.0 1.3 copy.71
  (122 shorter events, 5.5 us)
Async XLA Ops:
  7.2 6.4 %copy-start = (f32[16,9]{1,0:T(8,128)S(1)}, f32[16,9]{1,0:T(8,128)}, u32[]{:S(2)}) copy-start(f32[16,9]{1,0:T(8,128)} %param.10) | copy-start | bytes 1732
  7.2 85.1 %all-reduce.7.cloned.1.call-start = ((), (), s32[]{:S(2)}) async-start(), calls=%async_computation.2 | async-start | bytes 524288 | tf_op jit(solution)/shard_map/psum | solution.py:81
  8.4 27.7 %copy-start.5 = (bf16[32,32,2,128]{3,1,2,0:T(8,128)(2,1)}, bf16[32,32,2,128]{3,1,2,0:T(8,128)(2,1)S(1)}, u32[]{:S(2)}) copy-start(bf16[32,32,2,128]{3,1,2,0:T(8,128)(2,1)S(1)} %copy.53) | copy-start | bytes 1572868
  8.4 17.9 %collective-permute-start = (bf16[32,32,2,128]{3,1,2,0:T(8,128)(2,1)S(1)}, bf16[32,32,2,128]{3,1,2,0:T(8,128)(2,1)S(1)}, u32[]{:S(2)}, u32[]{:S(2)}) collective-permute-start(bf16[32,32,2,128]{3,1,2,0:T(8,128)(2,1)S(1)} %copy.53), channel_id=1, source_target_pairs={{0,4},{4,8},{8,12},{12,0},{1,5},{5,9},{9,13},{13,1},{2,6},{6,10},{... | collective-permute-start | bytes 1572872 | tf_op jit(solution)/shard_map/ppermute | solution.py:14
  11.5 24.6 %collective-permute-start.1 = (bf16[32,32,2,128]{3,1,2,0:T(8,128)(2,1)S(1)}, bf16[32,32,2,128]{3,1,2,0:T(8,128)(2,1)S(1)}, u32[]{:S(2)}, u32[]{:S(2)}) collective-permute-start(bf16[32,32,2,128]{3,1,2,0:T(8,128)(2,1)S(1)} %copy.53), channel_id=1, source_target_pairs={{4,0},{8,4},{12,8},{0,12},{5,1},{9,5},{13,9},{1,13},{6,2},{10,6},{... | collective-permute-start | bytes 1572872 | tf_op jit(solution)/shard_map/ppermute | solution.py:15
  14.6 6.0 %copy-start.48 = (f32[64]{0:T(128)}, f32[64]{0:T(128)S(1)}, u32[]{:S(2)}) copy-start(f32[64]{0:T(128)S(1)} %get-tuple-element.116) | copy-start | bytes 772
  26.3 9.8 %copy-start.7 = (bf16[32,32,2,128]{3,1,2,0:T(8,128)(2,1)}, bf16[32,32,2,128]{3,1,2,0:T(8,128)(2,1)S(1)}, u32[]{:S(2)}) copy-start(bf16[32,32,2,128]{3,1,2,0:T(8,128)(2,1)S(1)} %collective-permute-done) | copy-start | bytes 1572868
  38.9 7.3 %copy-start.4 = (f32[32,25]{1,0:T(8,128)S(1)}, f32[32,25]{1,0:T(8,128)}, u32[]{:S(2)}) copy-start(f32[32,25]{1,0:T(8,128)} %param.11) | copy-start | bytes 9604
  42.0 5.0 %collective-permute-start.2 = (bf16[32,32,6,2]{1,0,3,2:T(8,128)(2,1)}, bf16[32,32,6,2]{1,0,3,2:T(8,128)(2,1)}, u32[]{:S(2)}, u32[]{:S(2)}) collective-permute-start(bf16[32,32,6,2]{1,0,3,2:T(8,128)(2,1)} %copy.56), channel_id=1, source_target_pairs={{0,2},{2,0},{1,3},{3,1},{4,6},{6,4},{5,7},{7,5},{8,10},{10,8},{9,1... | collective-permute-start | bytes 73736 | tf_op jit(solution)/shard_map/ppermute | solution.py:14
  45.6 4.9 %collective-permute-start.3 = (bf16[32,32,6,2]{1,0,3,2:T(8,128)(2,1)}, bf16[32,32,6,2]{1,0,3,2:T(8,128)(2,1)}, u32[]{:S(2)}, u32[]{:S(2)}) collective-permute-start(bf16[32,32,6,2]{1,0,3,2:T(8,128)(2,1)} %copy.58), channel_id=1, source_target_pairs={{2,0},{0,2},{3,1},{1,3},{6,4},{4,6},{7,5},{5,7},{10,8},{8,10},{11,... | collective-permute-start | bytes 73736 | tf_op jit(solution)/shard_map/ppermute | solution.py:15
  49.2 15.6 %copy-start.1 = (bf16[32,32,6,2]{3,1,2,0:T(8,128)(2,1)}, bf16[32,32,6,2]{3,1,2,0:T(8,128)(2,1)S(1)}, u32[]{:S(2)}) copy-start(bf16[32,32,6,2]{3,1,2,0:T(8,128)(2,1)S(1)} %copy.57) | copy-start | bytes 73732
  64.7 7.2 %copy-start.39 = (f32[4,32]{1,0:T(4,128)S(1)}, f32[4,32]{1,0:T(4,128)}, u32[]{:S(2)}) copy-start(f32[4,32]{1,0:T(4,128)} %param.13) | copy-start | bytes 1540
  92.3 4.9 %copy-start.17 = (f32[16,64]{0,1:T(8,128)S(1)}, f32[16,64]{0,1:T(8,128)}, u32[]{:S(2)}) copy-start(f32[16,64]{0,1:T(8,128)} %get-tuple-element.132) | copy-start | bytes 12292
  92.3 4.9 %copy-start.18 = (f32[16,64]{0,1:T(8,128)S(1)}, f32[16,64]{0,1:T(8,128)}, u32[]{:S(2)}) copy-start(f32[16,64]{0,1:T(8,128)} %get-tuple-element.148) | copy-start | bytes 12292
  92.3 4.9 %copy-start.19 = (f32[16,64]{0,1:T(8,128)S(1)}, f32[16,64]{0,1:T(8,128)}, u32[]{:S(2)}) copy-start(f32[16,64]{0,1:T(8,128)} %get-tuple-element.136) | copy-start | bytes 12292
  92.3 4.9 %copy-start.20 = (f32[16,64]{0,1:T(8,128)S(1)}, f32[16,64]{0,1:T(8,128)}, u32[]{:S(2)}) copy-start(f32[16,64]{0,1:T(8,128)} %get-tuple-element.146) | copy-start | bytes 12292
  92.3 4.9 %copy-start.21 = (f32[16,64]{0,1:T(8,128)S(1)}, f32[16,64]{0,1:T(8,128)}, u32[]{:S(2)}) copy-start(f32[16,64]{0,1:T(8,128)} %get-tuple-element.140) | copy-start | bytes 12292
  92.3 4.9 %copy-start.22 = (f32[16,64]{0,1:T(8,128)S(1)}, f32[16,64]{0,1:T(8,128)}, u32[]{:S(2)}) copy-start(f32[16,64]{0,1:T(8,128)} %get-tuple-element.144) | copy-start | bytes 12292
  97.1 6.3 %copy-start.3 = (bf16[32,32,6,2]{3,1,2,0:T(8,128)(2,1)S(1)}, bf16[32,32,6,2]{3,1,2,0:T(8,128)(2,1)}, u32[]{:S(2)}) copy-start(bf16[32,32,6,2]{3,1,2,0:T(8,128)(2,1)} %copy.59) | copy-start | bytes 73732
  98.9 8.5 %copy-start.2 = (bf16[32,32,6,2]{3,1,2,0:T(8,128)(2,1)S(1)}, bf16[32,32,6,2]{3,1,2,0:T(8,128)(2,1)}, u32[]{:S(2)}) copy-start(bf16[32,32,6,2]{3,1,2,0:T(8,128)(2,1)} %copy-done.1) | copy-start | bytes 73732
  103.5 11.6 %copy-start.6 = (bf16[32,32,2,128]{3,1,2,0:T(8,128)(2,1)S(1)}, bf16[32,32,2,128]{3,1,2,0:T(8,128)(2,1)}, u32[]{:S(2)}) copy-start(bf16[32,32,2,128]{3,1,2,0:T(8,128)(2,1)} %copy-done.5) | copy-start | bytes 1572868
  103.5 11.6 %copy-start.8 = (bf16[32,32,2,128]{3,1,2,0:T(8,128)(2,1)S(1)}, bf16[32,32,2,128]{3,1,2,0:T(8,128)(2,1)}, u32[]{:S(2)}) copy-start(bf16[32,32,2,128]{3,1,2,0:T(8,128)(2,1)} %copy-done.7) | copy-start | bytes 1572868
  103.5 11.6 %copy-start.10 = (bf16[32,32,2,128]{3,1,2,0:T(8,128)(2,1)S(1)}, bf16[32,32,2,128]{3,1,2,0:T(8,128)(2,1)}, u32[]{:S(2)}) copy-start(bf16[32,32,2,128]{3,1,2,0:T(8,128)(2,1)} %copy-done.9) | copy-start | bytes 1572868
  103.5 11.6 %copy-start.11 = (bf16[32,32,2,128]{3,2,1,0:T(2,128)(2,1)S(1)}, bf16[32,32,2,128]{3,2,1,0:T(2,128)(2,1)}, u32[]{:S(2)}) copy-start(bf16[32,32,2,128]{3,2,1,0:T(2,128)(2,1)} %param.7) | copy-start | bytes 1572868
  103.5 11.6 %copy-start.14 = (bf16[32,32,2,128]{3,1,2,0:T(8,128)(2,1)S(1)}, bf16[32,32,2,128]{3,1,2,0:T(8,128)(2,1)}, u32[]{:S(2)}) copy-start(bf16[32,32,2,128]{3,1,2,0:T(8,128)(2,1)} %get-tuple-element.92) | copy-start | bytes 1572868
  103.5 11.6 %copy-start.15 = (bf16[32,32,2,128]{3,1,2,0:T(8,128)(2,1)S(1)}, bf16[32,32,2,128]{3,1,2,0:T(8,128)(2,1)}, u32[]{:S(2)}) copy-start(bf16[32,32,2,128]{3,1,2,0:T(8,128)(2,1)} %get-tuple-element.93) | copy-start | bytes 1572868
  107.4 8.8 %copy-start.16 = (f32[4,64,2,128]{3,0,2,1:T(4,128)S(1)}, f32[4,64,2,128]{3,0,2,1:T(4,128)}, u32[]{:S(2)}) copy-start(f32[4,64,2,128]{3,0,2,1:T(4,128)} %all-reduce.7.cloned.1.call-done) | copy-start | bytes 786436
  107.4 8.8 %copy-start.23 = (s32[64,2,128]{2,1,0:T(2,128)S(1)}, s32[64,2,128]{2,1,0:T(2,128)}, u32[]{:S(2)}) copy-start(s32[64,2,128]{2,1,0:T(2,128)} %param.8) | copy-start | bytes 196612
  111.2 38.7 %collective-permute-start.4 = (bf16[32,32,2,128]{3,1,2,0:T(8,128)(2,1)S(1)}, bf16[32,32,2,128]{3,1,2,0:T(8,128)(2,1)S(1)}, u32[]{:S(2)}, u32[]{:S(2)}) collective-permute-start(bf16[32,32,2,128]{3,1,2,0:T(8,128)(2,1)S(1)} %bitcast.136), channel_id=1, source_target_pairs={{0,4},{4,8},{8,12},{12,0},{1,5},{5,9},{9,13},{13,1},{2,6},{6,10},{... | collective-permute-start | bytes 1572872 | tf_op jit(solution)/shard_map/ppermute | solution.py:14
  113.0 37.7 %collective-permute-start.5 = (bf16[32,32,2,128]{3,1,2,0:T(8,128)(2,1)S(1)}, bf16[32,32,2,128]{3,1,2,0:T(8,128)(2,1)}, u32[]{:S(2)}, u32[]{:S(2)}) collective-permute-start(bf16[32,32,2,128]{3,1,2,0:T(8,128)(2,1)S(1)} %bitcast.137), channel_id=1, source_target_pairs={{4,0},{8,4},{12,8},{0,12},{5,1},{9,5},{13,9},{1,13},{6,2},{10,6},{... | collective-permute-start | bytes 1572872 | tf_op jit(solution)/shard_map/ppermute | solution.py:15
  154.5 13.5 %copy-start.13 = (bf16[32,32,2,128]{3,1,2,0:T(8,128)(2,1)S(1)}, bf16[32,32,2,128]{3,1,2,0:T(8,128)(2,1)}, u32[]{:S(2)}) copy-start(bf16[32,32,2,128]{3,1,2,0:T(8,128)(2,1)} %copy-done.12) | copy-start | bytes 1572868
  157.1 6.0 %collective-permute-start.6 = (bf16[32,32,6,2]{1,0,3,2:T(8,128)(2,1)S(1)}, bf16[32,32,6,2]{1,0,3,2:T(8,128)(2,1)S(1)}, u32[]{:S(2)}, u32[]{:S(2)}) collective-permute-start(bf16[32,32,6,2]{1,0,3,2:T(8,128)(2,1)S(1)} %copy.75), channel_id=1, source_target_pairs={{2,0},{0,2},{3,1},{1,3},{6,4},{4,6},{7,5},{5,7},{10,8},{8,10},{11,... | collective-permute-start | bytes 73736 | tf_op jit(solution)/shard_map/ppermute | solution.py:15
  161.1 4.7 %collective-permute-start.7 = (bf16[32,32,6,2]{1,0,3,2:T(8,128)(2,1)S(1)}, bf16[32,32,6,2]{1,0,3,2:T(8,128)(2,1)S(1)}, u32[]{:S(2)}, u32[]{:S(2)}) collective-permute-start(bf16[32,32,6,2]{1,0,3,2:T(8,128)(2,1)S(1)} %copy.76), channel_id=1, source_target_pairs={{0,2},{2,0},{1,3},{3,1},{4,6},{6,4},{5,7},{7,5},{8,10},{10,8},{9,1... | collective-permute-start | bytes 73736 | tf_op jit(solution)/shard_map/ppermute | solution.py:14
  168.0 4.4 %copy-start.24 = (f32[32]{0:T(128)S(1)}, f32[32]{0:T(128)}, u32[]{:S(2)}) copy-start(f32[32]{0:T(128)} %get-tuple-element.64) | copy-start | bytes 388
  168.0 4.4 %copy-start.25 = (f32[32]{0:T(128)S(1)}, f32[32]{0:T(128)}, u32[]{:S(2)}) copy-start(f32[32]{0:T(128)} %get-tuple-element.65) | copy-start | bytes 388
  168.0 4.4 %copy-start.26 = (f32[32]{0:T(128)S(1)}, f32[32]{0:T(128)}, u32[]{:S(2)}) copy-start(f32[32]{0:T(128)} %get-tuple-element.66) | copy-start | bytes 388
  168.0 4.4 %copy-start.27 = (f32[32]{0:T(128)S(1)}, f32[32]{0:T(128)}, u32[]{:S(2)}) copy-start(f32[32]{0:T(128)} %get-tuple-element.67) | copy-start | bytes 388
  168.0 4.4 %copy-start.28 = (f32[32]{0:T(128)S(1)}, f32[32]{0:T(128)}, u32[]{:S(2)}) copy-start(f32[32]{0:T(128)} %get-tuple-element.68) | copy-start | bytes 388
  168.1 4.4 %copy-start.29 = (f32[32]{0:T(128)S(1)}, f32[32]{0:T(128)}, u32[]{:S(2)}) copy-start(f32[32]{0:T(128)} %get-tuple-element.69) | copy-start | bytes 388
  168.1 4.4 %copy-start.30 = (f32[32]{0:T(128)S(1)}, f32[32]{0:T(128)}, u32[]{:S(2)}) copy-start(f32[32]{0:T(128)} %get-tuple-element.70) | copy-start | bytes 388
  168.1 4.4 %copy-start.31 = (f32[32]{0:T(128)S(1)}, f32[32]{0:T(128)}, u32[]{:S(2)}) copy-start(f32[32]{0:T(128)} %get-tuple-element.71) | copy-start | bytes 388
  168.1 4.4 %copy-start.32 = (f32[32]{0:T(128)S(1)}, f32[32]{0:T(128)}, u32[]{:S(2)}) copy-start(f32[32]{0:T(128)} %get-tuple-element.72) | copy-start | bytes 388
  168.1 4.4 %copy-start.33 = (f32[32]{0:T(128)S(1)}, f32[32]{0:T(128)}, u32[]{:S(2)}) copy-start(f32[32]{0:T(128)} %get-tuple-element.73) | copy-start | bytes 388
  168.1 4.4 %copy-start.34 = (f32[32]{0:T(128)S(1)}, f32[32]{0:T(128)}, u32[]{:S(2)}) copy-start(f32[32]{0:T(128)} %get-tuple-element.74) | copy-start | bytes 388
  168.1 4.4 %copy-start.35 = (f32[32]{0:T(128)S(1)}, f32[32]{0:T(128)}, u32[]{:S(2)}) copy-start(f32[32]{0:T(128)} %get-tuple-element.75) | copy-start | bytes 388
  168.1 4.4 %copy-start.36 = (f32[32]{0:T(128)S(1)}, f32[32]{0:T(128)}, u32[]{:S(2)}) copy-start(f32[32]{0:T(128)} %get-tuple-element.76) | copy-start | bytes 388
  168.1 4.4 %copy-start.37 = (f32[32]{0:T(128)S(1)}, f32[32]{0:T(128)}, u32[]{:S(2)}) copy-start(f32[32]{0:T(128)} %get-tuple-element.81) | copy-start | bytes 388
  168.1 4.4 %copy-start.38 = (f32[32]{0:T(128)S(1)}, f32[32]{0:T(128)}, u32[]{:S(2)}) copy-start(f32[32]{0:T(128)} %get-tuple-element.82) | copy-start | bytes 388
  (10 other events, 28.0 us)
Sparse Core Ops, SparseCore 0:
  73.5 18.7 all-reduce.6
